TPU v7x, 32 devices: a whole 2x2x4 slice. The times are simulated.
32 devices in a mesh: grp: 4 (over x, core), sub: 8 (over z, y).
Axes of the slice: x: 2, y: 2, z: 4, core: 2. Of those that a mesh axis runs over, the one named last changes fastest.
Arguments:
- loads: float32 [32, 8, 1024], P(('grp', 'sub')), may hold values from -6 to 6
- schur: bfloat16 [32, 1024, 1024], P(('grp', 'sub')), may hold values from -0.1875 to 0.1875
- neumann: bfloat16 [32, 1024, 1024], P(('grp', 'sub')), may hold values from -0.1875 to 0.1875
- basis: float32 [32, 24, 1024], P(('grp', 'sub')), may hold values from -0.375 to 0.375
- coarse_index: int32 [32, 24], P(('grp', 'sub')), may hold values from 0 to 127
- coarse_inverse: float32 [128, 128], P(('grp', 'sub')), may hold values from -1 to 3
Outputs:
- solution: float32 [32, 8, 1024], P(('grp', 'sub'))
- residual: float32 [32, 8, 1024], P(('grp', 'sub'))
All inputs are finite; a program needn't handle non-finite values.
Results may differ from a plain program's by a relative error of at most 0.00063.
Values sent between devices are 32-bit elements; how exact they have to be, the bound alone decides.
A program may use at most 64 MiB of HBM per device.

v0:
```python
import jax
import jax.numpy as jnp
from jax import lax
from jax.sharding import PartitionSpec as P

RIM = 256


def with_halo(x, sides, width):
    for axis, dim in sides:
        peers, length = (lax.axis_size(axis), x.shape[dim])
        up = [(i, (i + 1) % peers) for i in range(peers - 1)]
        down = [(j, i) for i, j in up]
        last = lax.slice_in_dim(x, length - width, length, axis=dim)
        first = lax.slice_in_dim(x, 0, width, axis=dim)
        before = lax.ppermute(last, axis, up)
        after = lax.ppermute(first, axis, down)
        x = jnp.concatenate([before, x, after], axis=dim)
    return x


def local(loads, schur, neumann, basis, coarse_index, coarse_inverse):
    width = loads.shape[2]
    coarse_total = coarse_inverse.shape[1]
    high = lax.Precision.HIGHEST
    position = lax.axis_index("sub")
    final_index = lax.axis_size("sub") - 1
    columns = lax.broadcasted_iota(jnp.int32, (1, 1, width), 2)
    lower_rim = (columns < RIM) & (position > 0)
    upper_rim = (columns >= width - RIM) & (position < final_index)
    weights = jnp.where(lower_rim | upper_rim, 0.5, 1.0).astype(jnp.float32)
    selector = (
        coarse_index[0][:, None] == lax.broadcasted_iota(jnp.int32, (1, coarse_total), 1)
    ).astype(jnp.float32)

    def assemble(field):
        padded = with_halo(field, (("sub", 2),), RIM)
        from_left = padded[:, :, :RIM]
        from_right = padded[:, :, RIM + width :]
        middle = field[:, :, RIM : width - RIM]
        return jnp.concatenate(
            [field[:, :, :RIM] + from_left, middle, field[:, :, width - RIM :] + from_right], axis=2
        )

    force = assemble(loads)
    residual = force
    weighted = (weights * residual)[0]
    product = jnp.dot(weighted.astype(jnp.bfloat16), neumann[0], preferred_element_type=jnp.float32)
    neumann_part = 0.25 * weighted + 0.0625 * product
    coarse_terms = jnp.dot(weighted, basis[0].T, precision=high)
    partial_sums = jnp.dot(coarse_terms, selector, precision=high)
    owned = lax.psum_scatter(partial_sums, ("grp", "sub"), scatter_dimension=1, tiled=True)
    value_terms = jnp.dot(owned, coarse_inverse, precision=high)
    within = lax.psum(value_terms, "sub")
    coarse_value = lax.psum(within, "grp")
    picked = jnp.dot(coarse_value, selector.T, precision=high)
    combined = neumann_part + jnp.dot(picked, basis[0], precision=high)
    solution = assemble(weights * combined[None])
    product = jnp.dot(
        solution[0].astype(jnp.bfloat16), schur[0], preferred_element_type=jnp.float32
    )
    residual = force - assemble((4.0 * solution[0] + product)[None])
    return (solution, residual)


def solution(mesh):
    in_specs = (
        P(("grp", "sub"), None, None),
        P(("grp", "sub"), None, None),
        P(("grp", "sub"), None, None),
        P(("grp", "sub"), None, None),
        P(("grp", "sub"), None),
        P(("grp", "sub"), None),
    )
    out_specs = (P(("grp", "sub"), None, None), P(("grp", "sub"), None, None))
    return jax.shard_map(local, mesh=mesh, in_specs=in_specs, out_specs=out_specs, check_vma=False)
```

profile of v0, /device:TPU:0, one launch (start us, length us, event | category | flops | bytes accessed | tf_op | source)
XLA Modules:
  0.0 103.4 jit_solution(9314330173535048265)
XLA Ops:
  0.6 0.0 copy-start
  0.6 0.9 fusion.53
  1.5 4.9 %collective-permute-start = (f32[1,8,256]{2,1,0:T(8,128)S(1)}, f32[1,8,256]{2,1,0:T(8,128)S(1)}, u32[]{:S(2)}, u32[]{:S(2)}) collective-permute-start(f32[1,8,256]{2,1,0:T(8,128)S(1)} %get-tuple-element.18), channel_id=1, source_target_pairs={{0,1},{1,2},{2,3},{3,4},{4,5},{5,6},{6,7},{8,9},{9,10},{10,11},{11... | collective-permute-start | bytes 24584 | tf_op jit(solution)/shard_map/ppermute | solution.py:16
  6.4 1.3 %collective-permute-start.1 = (f32[1,8,256]{2,1,0:T(8,128)S(1)}, f32[1,8,256]{2,1,0:T(8,128)S(1)}, u32[]{:S(2)}, u32[]{:S(2)}) collective-permute-start(f32[1,8,256]{2,1,0:T(8,128)S(1)} %get-tuple-element.19), channel_id=1, source_target_pairs={{1,0},{2,1},{3,2},{4,3},{5,4},{6,5},{7,6},{9,8},{10,9},{11,10},{12... | collective-permute-start | bytes 24584 | tf_op jit(solution)/shard_map/ppermute | solution.py:17
  7.7 0.7 fusion.51
  8.4 0.0 collective-permute-done
  8.4 3.5 %collective-permute-done.1 = f32[1,8,256]{2,1,0:T(8,128)S(1)} collective-permute-done((f32[1,8,256]{2,1,0:T(8,128)S(1)}, f32[1,8,256]{2,1,0:T(8,128)S(1)}, u32[]{:S(2)}, u32[]{:S(2)}) %collective-permute-start.1) | collective-permute-done | bytes 8224 | tf_op jit(solution)/shard_map/ppermute | solution.py:17
  11.9 0.7 slice_add_fusion.5
  12.6 1.1 %fusion.21 = f32[8,24]{1,0:T(8,128)S(1)} fusion(f32[1,24,1024]{2,1,0:T(8,128)} %param.9, f32[8,256]{1,0:T(8,128)S(1)} %bitcast.50, f32[8,512]{1,0:T(8,128)S(1)} %get-tuple-element.11, f32[8,256]{1,0:T(8,128)S(1)} %bitcast.48, f32[1024]{0:T(1024)S(1)} %fusion.44), kind=kOutput, calls=%fused_computation.11 | convolution fusion | flops 2383872 | bytes 135936 | tf_op jit(solution)/shard_map/dot_general | solution.py:50
  13.7 0.9 fusion.37
  14.6 41.4 %all-reduce = f32[8,128]{1,0:T(8,128)S(1)} all-reduce(f32[8,128]{1,0:T(8,128)S(1)} %fusion.37), channel_id=2, replica_groups=mesh['grp'=4,'sub'=8] {'grp','sub'}, use_global_device_ids=true, to_apply=%region_0.1.clone | all-reduce | flops 1024 | bytes 8192
  56.0 0.9 fusion.40
  56.9 21.1 %psum.14 = f32[8,128]{1,0:T(8,128)S(1)} all-reduce(f32[8,128]{1,0:T(8,128)S(1)} %fusion.40), channel_id=1, replica_groups=mesh['grp'=4,'sub'=8] {'sub'}, use_global_device_ids=true, to_apply=%region_1.2 | all-reduce | flops 1024 | bytes 8192 | tf_op jit(solution)/shard_map/psum | solution.py:54
  78.0 5.8 %psum.15 = f32[8,128]{1,0:T(8,128)S(1)} all-reduce(f32[8,128]{1,0:T(8,128)S(1)} %psum.14), channel_id=1, replica_groups=mesh['grp'=4,'sub'=8] {'grp'}, use_global_device_ids=true, to_apply=%region_2.3 | all-reduce | flops 1024 | bytes 8192 | tf_op jit(solution)/shard_map/psum | solution.py:55
  83.8 0.0 copy-start.1
  83.8 1.0 fusion.36
  84.8 1.1 %fusion.19 = f32[8,1024]{1,0:T(8,128)S(1)} fusion(f32[8,24]{1,0:T(8,128)S(1)} %fusion.36, f32[1,24,1024]{2,1,0:T(8,128)} %param.9), kind=kOutput, calls=%fused_computation.9 | convolution fusion | flops 2359296 | bytes 131840 | tf_op jit(solution)/shard_map/dot_general | solution.py:57
  85.9 0.0 copy-done
  85.9 0.4 fusion.16
  86.3 1.3 %collective-permute-start.2 = (f32[1,8,256]{2,1,0:T(8,128)S(1)}, f32[1,8,256]{2,1,0:T(8,128)S(1)}, u32[]{:S(2)}, u32[]{:S(2)}) collective-permute-start(f32[1,8,256]{2,1,0:T(8,128)S(1)} %get-tuple-element.14), channel_id=1, source_target_pairs={{0,1},{1,2},{2,3},{3,4},{4,5},{5,6},{6,7},{8,9},{9,10},{10,11},{11... | collective-permute-start | bytes 24584 | tf_op jit(solution)/shard_map/ppermute | solution.py:16
  87.6 1.3 %collective-permute-start.3 = (f32[1,8,256]{2,1,0:T(8,128)S(1)}, f32[1,8,256]{2,1,0:T(8,128)S(1)}, u32[]{:S(2)}, u32[]{:S(2)}) collective-permute-start(f32[1,8,256]{2,1,0:T(8,128)S(1)} %get-tuple-element.15), channel_id=1, source_target_pairs={{1,0},{2,1},{3,2},{4,3},{5,4},{6,5},{7,6},{9,8},{10,9},{11,10},{12... | collective-permute-start | bytes 24584 | tf_op jit(solution)/shard_map/ppermute | solution.py:17
  88.9 0.0 collective-permute-done.2
  88.9 4.2 %collective-permute-done.3 = f32[1,8,256]{2,1,0:T(8,128)S(1)} collective-permute-done((f32[1,8,256]{2,1,0:T(8,128)S(1)}, f32[1,8,256]{2,1,0:T(8,128)S(1)}, u32[]{:S(2)}, u32[]{:S(2)}) %collective-permute-start.3) | collective-permute-done | bytes 8224 | tf_op jit(solution)/shard_map/ppermute | solution.py:17
  93.2 0.0 copy-start.2
  93.2 0.0 copy-done.1
  93.2 0.4 fusion.23
  93.6 3.6 %collective-permute-start.4 = (f32[1,8,256]{2,1,0:T(8,128)S(1)}, f32[1,8,256]{2,1,0:T(8,128)S(1)}, u32[]{:S(2)}, u32[]{:S(2)}) collective-permute-start(f32[1,8,256]{2,1,0:T(8,128)S(1)} %get-tuple-element.8), channel_id=1, source_target_pairs={{0,1},{1,2},{2,3},{3,4},{4,5},{5,6},{6,7},{8,9},{9,10},{10,11},{11... | collective-permute-start | bytes 24584 | tf_op jit(solution)/shard_map/ppermute | solution.py:16
  97.2 1.3 %collective-permute-start.5 = (f32[1,8,256]{2,1,0:T(8,128)S(1)}, f32[1,8,256]{2,1,0:T(8,128)S(1)}, u32[]{:S(2)}, u32[]{:S(2)}) collective-permute-start(f32[1,8,256]{2,1,0:T(8,128)S(1)} %get-tuple-element.9), channel_id=1, source_target_pairs={{1,0},{2,1},{3,2},{4,3},{5,4},{6,5},{7,6},{9,8},{10,9},{11,10},{12... | collective-permute-start | bytes 24584 | tf_op jit(solution)/shard_map/ppermute | solution.py:17
  98.5 0.0 collective-permute-done.4
  98.6 4.2 %collective-permute-done.5 = f32[1,8,256]{2,1,0:T(8,128)S(1)} collective-permute-done((f32[1,8,256]{2,1,0:T(8,128)S(1)}, f32[1,8,256]{2,1,0:T(8,128)S(1)}, u32[]{:S(2)}, u32[]{:S(2)}) %collective-permute-start.5) | collective-permute-done | bytes 8224 | tf_op jit(solution)/shard_map/ppermute | solution.py:17
  102.8 0.6 maximum_subtract_fusion
  103.4 0.0 copy-done.2
  (9 shorter events, 0.0 us)
Async XLA Ops:
  0.6 85.3 %copy-start = (bf16[1,1024,1024]{2,1,0:T(8,128)(2,1)S(1)}, bf16[1,1024,1024]{2,1,0:T(8,128)(2,1)}, u32[]{:S(2)}) copy-start(bf16[1,1024,1024]{2,1,0:T(8,128)(2,1)} %param.8) | copy-start | bytes 6291460
  1.5 6.9 %collective-permute-start = (f32[1,8,256]{2,1,0:T(8,128)S(1)}, f32[1,8,256]{2,1,0:T(8,128)S(1)}, u32[]{:S(2)}, u32[]{:S(2)}) collective-permute-start(f32[1,8,256]{2,1,0:T(8,128)S(1)} %get-tuple-element.18), channel_id=1, source_target_pairs={{0,1},{1,2},{2,3},{3,4},{4,5},{5,6},{6,7},{8,9},{9,10},{10,11},{11... | collective-permute-start | bytes 24584 | tf_op jit(solution)/shard_map/ppermute | solution.py:16
  6.4 5.5 %collective-permute-start.1 = (f32[1,8,256]{2,1,0:T(8,128)S(1)}, f32[1,8,256]{2,1,0:T(8,128)S(1)}, u32[]{:S(2)}, u32[]{:S(2)}) collective-permute-start(f32[1,8,256]{2,1,0:T(8,128)S(1)} %get-tuple-element.19), channel_id=1, source_target_pairs={{1,0},{2,1},{3,2},{4,3},{5,4},{6,5},{7,6},{9,8},{10,9},{11,10},{12... | collective-permute-start | bytes 24584 | tf_op jit(solution)/shard_map/ppermute | solution.py:17
  83.8 9.3 %copy-start.1 = (bf16[1,1024,1024]{2,1,0:T(8,128)(2,1)S(1)}, bf16[1,1024,1024]{2,1,0:T(8,128)(2,1)}, u32[]{:S(2)}) copy-start(bf16[1,1024,1024]{2,1,0:T(8,128)(2,1)} %param.7) | copy-start | bytes 6291460
  86.3 2.6 %collective-permute-start.2 = (f32[1,8,256]{2,1,0:T(8,128)S(1)}, f32[1,8,256]{2,1,0:T(8,128)S(1)}, u32[]{:S(2)}, u32[]{:S(2)}) collective-permute-start(f32[1,8,256]{2,1,0:T(8,128)S(1)} %get-tuple-element.14), channel_id=1, source_target_pairs={{0,1},{1,2},{2,3},{3,4},{4,5},{5,6},{6,7},{8,9},{9,10},{10,11},{11... | collective-permute-start | bytes 24584 | tf_op jit(solution)/shard_map/ppermute | solution.py:16
  87.6 5.5 %collective-permute-start.3 = (f32[1,8,256]{2,1,0:T(8,128)S(1)}, f32[1,8,256]{2,1,0:T(8,128)S(1)}, u32[]{:S(2)}, u32[]{:S(2)}) collective-permute-start(f32[1,8,256]{2,1,0:T(8,128)S(1)} %get-tuple-element.15), channel_id=1, source_target_pairs={{1,0},{2,1},{3,2},{4,3},{5,4},{6,5},{7,6},{9,8},{10,9},{11,10},{12... | collective-permute-start | bytes 24584 | tf_op jit(solution)/shard_map/ppermute | solution.py:17
  93.2 10.2 %copy-start.2 = (f32[1,8,1024]{2,1,0:T(8,128)}, f32[1,8,1024]{2,1,0:T(8,128)S(1)}, u32[]{:S(2)}) copy-start(f32[1,8,1024]{2,1,0:T(8,128)S(1)} %pad_maximum_fusion) | copy-start | bytes 98308
  93.6 5.0 %collective-permute-start.4 = (f32[1,8,256]{2,1,0:T(8,128)S(1)}, f32[1,8,256]{2,1,0:T(8,128)S(1)}, u32[]{:S(2)}, u32[]{:S(2)}) collective-permute-start(f32[1,8,256]{2,1,0:T(8,128)S(1)} %get-tuple-element.8), channel_id=1, source_target_pairs={{0,1},{1,2},{2,3},{3,4},{4,5},{5,6},{6,7},{8,9},{9,10},{10,11},{11... | collective-permute-start | bytes 24584 | tf_op jit(solution)/shard_map/ppermute | solution.py:16
  97.2 5.5 %collective-permute-start.5 = (f32[1,8,256]{2,1,0:T(8,128)S(1)}, f32[1,8,256]{2,1,0:T(8,128)S(1)}, u32[]{:S(2)}, u32[]{:S(2)}) collective-permute-start(f32[1,8,256]{2,1,0:T(8,128)S(1)} %get-tuple-element.9), channel_id=1, source_target_pairs={{1,0},{2,1},{3,2},{4,3},{5,4},{6,5},{7,6},{9,8},{10,9},{11,10},{12... | collective-permute-start | bytes 24584 | tf_op jit(solution)/shard_map/ppermute | solution.py:17
where the time goes:
time: 104 us; the launch traced here: 103 us
  blocking collectives  68.4 us (66%)
  starting transfers between devices  13.7 us (13%)
  waiting for transfers between devices  12 us (12%)
  matrix products  5.65 us (5%)
  local copies, waits for them, and re-layouts  1.63 us (2%)
  other arithmetic  1.36 us (1%)
    unnamed x1, blocking collectives  41.4 us
    psum x1, blocking collectives, local(): within = lax.psum(value_terms, 'sub')  21.1 us
    ppermute x3, waiting for transfers between devices, with_halo(): after = lax.ppermute(first, axis, down)  11.9 us
    ppermute x3, starting transfers between devices, with_halo(): before = lax.ppermute(last, axis, up)  9.78 us
    psum x1, blocking collectives, local(): coarse_value = lax.psum(within, 'grp')  5.84 us
    ppermute x3, starting transfers between devices, with_halo(): after = lax.ppermute(first, axis, down)  3.88 us
  transfers between devices with their start and end apart: 6, of which 3 were waited for; matrix products, arithmetic and copies ran while one was open for 1% of the time, Pallas kernels for 0%

commit v1 on v0

--- a/solution.py
+++ b/solution.py
@@ -1,9 +1,316 @@
+import functools
+
 import jax
 import jax.numpy as jnp
 from jax import lax
+from jax.experimental import pallas as pl
+from jax.experimental.pallas import tpu as pltpu
 from jax.sharding import PartitionSpec as P
 
 RIM = 256
+MESH = pl.DeviceIdType.MESH
+GATHERED_LIMIT = 1 << 20
+BF16 = jnp.bfloat16
+F32 = jnp.float32
+NN = (((1,), (0,)), ((), ()))
+NT = (((1,), (1,)), ((), ()))
+
+
+def split(x):
+    high = x.astype(BF16)
+    return high, (x - high.astype(F32)).astype(BF16)
+
+
+def dot(a, b, dims=NN):
+    return lax.dot_general(a, b, dims, preferred_element_type=F32)
+
+
+def thin_dot(a, b_high, b_low, dims=NN):
+    rows = a.shape[0]
+    high, low = split(a)
+    both = dot(jnp.concatenate([high, low], axis=0), b_high, dims)
+    return both[:rows] + both[rows:] + dot(high, b_low, dims)
+
+
+def kernel(
+    n_grp, n_sub,
+    loads_hbm, schur_hbm, neumann_hbm, basis_hbm, index_hbm, inverse_hbm,
+    solution_hbm, residual_hbm,
+    loads, schur, neumann, basis, index, inverse_parts, inverse,
+    loads_in, basis_in, index_in, part_in, result_in,
+    e_high, e_low, h_high, h_low, part, result, solution, residual,
+    terms, terms_grp, group_terms, terms_sub,
+    local_sem, halo_send, halo_recv, grp_send, grp_recv, sub_send, sub_recv,
+    inv_sub_send, inv_sub_recv, inv_grp_send, inv_grp_recv,
+):
+    width = loads.shape[1]
+    coarse = inverse.shape[0]
+    rows = inverse_parts.shape[2]
+    g = lax.axis_index("grp")
+    b = lax.axis_index("sub")
+    grp_peers = [lax.rem(g + k, n_grp) for k in range(1, n_grp)]
+    sub_peers = [lax.rem(b + k, n_sub) for k in range(1, n_sub)]
+    has_left = b > 0
+    has_right = b < n_sub - 1
+    first = pl.ds(0, RIM)
+    last = pl.ds(width - RIM, RIM)
+
+    barrier = pltpu.get_barrier_semaphore()
+    for peer in sub_peers:
+        pl.semaphore_signal(barrier, inc=1, device_id=(g, peer), device_id_type=MESH)
+    for peer in grp_peers:
+        pl.semaphore_signal(barrier, inc=1, device_id=(peer, b), device_id_type=MESH)
+
+    def fetch(source, target, at):
+        copy = pltpu.make_async_copy(source, target, local_sem.at[at])
+        copy.start()
+        return copy
+
+    loads_copy = fetch(loads_hbm.at[0], loads, 0)
+    basis_copy = fetch(basis_hbm.at[0], basis, 1)
+    index_copy = fetch(index_hbm, index, 2)
+    inverse_copy = fetch(inverse_hbm, inverse_parts.at[g, b], 3)
+    neumann_copy = fetch(neumann_hbm.at[0], neumann, 4)
+    schur_copy = fetch(schur_hbm.at[0], schur, 5)
+
+    def remote(source, target, send, recv, device):
+        return pltpu.make_async_remote_copy(
+            src_ref=source, dst_ref=target, send_sem=send, recv_sem=recv,
+            device_id=device, device_id_type=MESH,
+        )
+
+    left_id = (g, lax.max(b - 1, 0))
+    right_id = (g, lax.min(b + 1, n_sub - 1))
+
+    def halo(lower, upper, landing, at):
+        to_right = remote(upper, landing.at[0], halo_send.at[at, 0], halo_recv.at[at, 0], right_id)
+        to_left = remote(lower, landing.at[1], halo_send.at[at, 1], halo_recv.at[at, 1], left_id)
+
+        def start():
+            pl.when(has_right)(lambda: to_right.start())
+            pl.when(has_left)(lambda: to_left.start())
+
+        def wait_recv():
+            pl.when(has_left)(lambda: to_right.wait_recv())
+            pl.when(has_right)(lambda: to_left.wait_recv())
+
+        def wait_send():
+            pl.when(has_right)(lambda: to_right.wait_send())
+            pl.when(has_left)(lambda: to_left.wait_send())
+
+        return start, wait_recv, wait_send
+
+    def clear(slot):
+        loads_in[slot] = jnp.zeros(loads_in.shape[1:], F32)
+        basis_in[slot] = jnp.zeros(basis_in.shape[1:], F32)
+        index_in[slot] = jnp.zeros(index_in.shape[1:], jnp.int32)
+        part_in[slot] = jnp.zeros(part_in.shape[1:], F32)
+        result_in[slot] = jnp.zeros(result_in.shape[1:], F32)
+
+    pl.when(jnp.logical_not(has_left))(lambda: clear(0))
+    pl.when(jnp.logical_not(has_right))(lambda: clear(1))
+
+    loads_halo = halo(loads.at[:, first], loads.at[:, last], loads_in, 0)
+    basis_halo = halo(basis.at[:, first], basis.at[:, last], basis_in, 1)
+    index_halo = halo(index, index, index_in, 2)
+    part_halo = halo(part.at[:, first], part.at[:, last], part_in, 3)
+    result_halo = halo(result.at[:, first], result.at[:, last], result_in, 4)
+
+    loads_copy.wait()
+    pl.semaphore_wait(barrier, n_grp + n_sub - 2)
+    loads_halo[0]()
+    index_copy.wait()
+    index_halo[0]()
+    basis_copy.wait()
+    basis_halo[0]()
+    inverse_copy.wait()
+    inv_sub = [
+        remote(inverse_parts.at[g, b], inverse_parts.at[g, b], inv_sub_send.at[k], inv_sub_recv.at[k], (g, peer))
+        for k, peer in enumerate(sub_peers)
+    ]
+    for copy in inv_sub:
+        copy.start()
+
+    def expand(index_row, functions):
+        place = lax.broadcasted_iota(jnp.int32, (coarse, index_row.shape[1]), 0)
+        chosen = jnp.where(place == index_row, 1.0, 0.0).astype(BF16)
+        high, low = split(functions)
+        return dot(chosen, high) + dot(chosen, low)
+
+    columns = lax.broadcasted_iota(jnp.int32, (1, width), 1)
+    shared = ((columns < RIM) & has_left) | ((columns >= width - RIM) & has_right)
+    weights = jnp.where(shared, 0.5, 1.0).astype(F32)
+
+    expanded = expand(index[...], basis[...])
+    high, low = split(expanded)
+    e_high[...] = high
+    e_low[...] = low
+
+    loads_halo[1]()
+
+    def assembled(field, landed):
+        return jnp.concatenate(
+            [field[:, :RIM] + landed[0], field[:, RIM : width - RIM], field[:, width - RIM :] + landed[1]], axis=1
+        )
+
+    force = assembled(loads[...], loads_in)
+    weighted = weights * force
+    terms[...] = thin_dot(weighted, e_high[...], e_low[...], NT)
+    to_grp = [
+        remote(terms, terms_grp.at[k], grp_send.at[k], grp_recv.at[k], (peer, b))
+        for k, peer in enumerate(grp_peers)
+    ]
+    for copy in to_grp:
+        copy.start()
+
+    neumann_copy.wait()
+    rounded = weighted.astype(BF16)
+
+    def neumann_columns(at, size):
+        product = dot(rounded, neumann[:, at : at + size])
+        here = weighted[:, at : at + size]
+        part[:, at : at + size] = weights[:, at : at + size] * (0.25 * here + 0.0625 * product)
+
+    neumann_columns(0, RIM)
+    neumann_columns(width - RIM, RIM)
+    part_halo[0]()
+
+    total = terms[...]
+    for k, copy in enumerate(to_grp):
+        copy.wait_recv()
+        total = total + terms_grp[k]
+    group_terms[...] = total
+    to_sub = [
+        remote(group_terms, terms_sub.at[k], sub_send.at[k], sub_recv.at[k], (g, peer))
+        for k, peer in enumerate(sub_peers)
+    ]
+    for copy in to_sub:
+        copy.start()
+
+    for copy in inv_sub:
+        copy.wait_recv()
+    inv_grp = [
+        remote(inverse_parts.at[g], inverse_parts.at[g], inv_grp_send.at[k], inv_grp_recv.at[k], (peer, b))
+        for k, peer in enumerate(grp_peers)
+    ]
+    for copy in inv_grp:
+        copy.start()
+
+    neumann_columns(RIM, width - 2 * RIM)
+
+    basis_halo[1]()
+    index_halo[1]()
+    own = weights * (e_high[...].astype(F32) + e_low[...].astype(F32))
+    from_left = own[:, :RIM] + 0.5 * expand(index_in[0], basis_in[0])
+    from_right = own[:, width - RIM :] + 0.5 * expand(index_in[1], basis_in[1])
+    f_high, f_low = split(jnp.concatenate([from_left, own[:, RIM : width - RIM], from_right], axis=1))
+    for copy in inv_grp:
+        copy.wait_recv()
+    for i in range(n_grp):
+        for j in range(n_sub):
+            at = (i * n_sub + j) * rows
+            inverse[at : at + rows, :] = inverse_parts[i, j]
+    i_high, i_low = split(inverse[...])
+    h = dot(i_high, f_high) + dot(i_high, f_low) + dot(i_low, f_high)
+    high, low = split(h)
+    h_high[...] = high
+    h_low[...] = low
+
+    part_halo[1]()
+    base = assembled(part[...], part_in)
+
+    total = group_terms[...]
+    for k, copy in enumerate(to_sub):
+        copy.wait_recv()
+        total = total + terms_sub[k]
+    found = base + thin_dot(total, h_high[...], h_low[...])
+    solution[...] = found
+    solution_copy = pltpu.make_async_copy(solution, solution_hbm.at[0], local_sem.at[6])
+    solution_copy.start()
+
+    schur_copy.wait()
+    rounded_solution = found.astype(BF16)
+
+    def schur_columns(at, size):
+        product = dot(rounded_solution, schur[:, at : at + size])
+        return 4.0 * found[:, at : at + size] + product
+
+    low_rim = schur_columns(0, RIM)
+    high_rim = schur_columns(width - RIM, RIM)
+    result[:, :RIM] = low_rim
+    result[:, width - RIM :] = high_rim
+    result_halo[0]()
+    residual[:, RIM : width - RIM] = force[:, RIM : width - RIM] - schur_columns(RIM, width - 2 * RIM)
+    for copy in inv_sub + inv_grp + to_grp + to_sub:
+        copy.wait_send()
+    for each in (loads_halo, basis_halo, index_halo, part_halo):
+        each[2]()
+    result_halo[1]()
+    residual[:, :RIM] = force[:, :RIM] - (low_rim + result_in[0])
+    residual[:, width - RIM :] = force[:, width - RIM :] - (high_rim + result_in[1])
+    residual_copy = pltpu.make_async_copy(residual, residual_hbm.at[0], local_sem.at[7])
+    residual_copy.start()
+    result_halo[2]()
+    solution_copy.wait()
+    residual_copy.wait()
+
+
+def fused(loads, schur, neumann, basis, coarse_index, coarse_inverse):
+    n_grp, n_sub = lax.axis_size("grp"), lax.axis_size("sub")
+    _, cases, width = loads.shape
+    corners = basis.shape[1]
+    rows, coarse = coarse_inverse.shape
+    dma = pltpu.SemaphoreType.DMA
+    field = pltpu.VMEM((cases, width), F32)
+    rims = pltpu.VMEM((2, cases, RIM), F32)
+    scratch = [
+        field,
+        pltpu.VMEM((width, width), BF16),
+        pltpu.VMEM((width, width), BF16),
+        pltpu.VMEM((corners, width), F32),
+        pltpu.VMEM((1, corners), jnp.int32),
+        pltpu.VMEM((n_grp, n_sub, rows, coarse), F32),
+        pltpu.VMEM((coarse, coarse), F32),
+        rims,
+        pltpu.VMEM((2, corners, RIM), F32),
+        pltpu.VMEM((2, 1, corners), jnp.int32),
+        rims,
+        rims,
+        pltpu.VMEM((coarse, width), BF16),
+        pltpu.VMEM((coarse, width), BF16),
+        pltpu.VMEM((coarse, width), BF16),
+        pltpu.VMEM((coarse, width), BF16),
+        field,
+        field,
+        field,
+        field,
+        pltpu.VMEM((cases, coarse), F32),
+        pltpu.VMEM((n_grp - 1, cases, coarse), F32),
+        pltpu.VMEM((cases, coarse), F32),
+        pltpu.VMEM((n_sub - 1, cases, coarse), F32),
+        dma((8,)),
+        dma((5, 2)),
+        dma((5, 2)),
+        dma((n_grp - 1,)),
+        dma((n_grp - 1,)),
+        dma((n_sub - 1,)),
+        dma((n_sub - 1,)),
+        dma((n_sub - 1,)),
+        dma((n_sub - 1,)),
+        dma((n_grp - 1,)),
+        dma((n_grp - 1,)),
+    ]
+    out = jax.ShapeDtypeStruct(loads.shape, F32)
+    return pl.pallas_call(
+        functools.partial(kernel, n_grp, n_sub),
+        out_shape=(out, out),
+        in_specs=[pl.BlockSpec(memory_space=pl.ANY)] * 6,
+        out_specs=(pl.BlockSpec(memory_space=pl.ANY),) * 2,
+        scratch_shapes=scratch,
+        compiler_params=pltpu.CompilerParams(
+            collective_id=0, has_side_effects=True, vmem_limit_bytes=48 << 20
+        ),
+    )(loads, schur, neumann, basis, coarse_index, coarse_inverse)
 
 
 def with_halo(x, sides, width):
@@ -19,7 +326,7 @@
     return x
 
 
-def local(loads, schur, neumann, basis, coarse_index, coarse_inverse):
+def staged(loads, schur, neumann, basis, coarse_index, coarse_inverse):
     width = loads.shape[2]
     coarse_total = coarse_inverse.shape[1]
     high = lax.Precision.HIGHEST
@@ -63,6 +370,12 @@
     return (solution, residual)
 
 
+def local(loads, schur, neumann, basis, coarse_index, coarse_inverse):
+    coarse_total = coarse_inverse.shape[1]
+    form = fused if 4 * coarse_total * coarse_total <= GATHERED_LIMIT else staged
+    return form(loads, schur, neumann, basis, coarse_index, coarse_inverse)
+
+
 def solution(mesh):
     in_specs = (
         P(("grp", "sub"), None, None),

time: 104 us -> 27.3 us (0.26)
  blocking collectives: 68.4 us -> 0 us
  Pallas kernels: 0 us -> 19 us
  starting transfers between devices: 13.7 us -> 0 us
  waiting for transfers between devices: 12 us -> 0 us
  local copies, waits for them, and re-layouts: 1.63 us -> 7.39 us
  matrix products: 5.65 us -> 0 us
  other arithmetic: 1.36 us -> 0 us
    unnamed x1 -> x0, blocking collectives: 41.4 us -> none
    psum x2 -> x0, blocking collectives: 26.9 us -> none  [the longest x1 21.1 us: local(): within = lax.psum(value_terms, 'sub')]
    pallas_call x0 -> x1, Pallas kernels: none -> 19 us  [fused(): pl.pallas_call(functools.partial(kernel, n_grp, n_sub), out_shape=(out, o...]
    ppermute x6 -> x0, starting transfers between devices: 13.7 us -> none  [the longest x3 9.78 us: with_halo(): before = lax.ppermute(last, axis, up)]
    ppermute x6 -> x0, waiting for transfers between devices: 12 us -> none  [the longest x3 11.9 us: with_halo(): after = lax.ppermute(first, axis, down)]
    unnamed x6 -> x14, local copies, waits for them, and re-layouts: 0.02 us -> 7.39 us
    dot_general x7 -> x0, matrix products: 5.65 us -> none  [the longest x1 1.07 us: local(): combined = neumann_part + jnp.dot(picked, basis[0], precision=high)]
    slice x6 -> x0, local copies, waits for them, and re-layouts: 1.61 us -> none  [the longest x3 0.88 us: with_halo(): last = lax.slice_in_dim(x, length - width, length, axis=dim)]
  transfers between devices with their start and end apart: 6 -> 0, of which waited for: 3 -> 0; matrix products, arithmetic and copies ran while one was open for 1% -> 0% of each run, Pallas kernels for 0% -> 0%
where the time goes in v1:
time: 27.3 us; the launch traced here: 27 us
  Pallas kernels  19 us (70%)
  local copies, waits for them, and re-layouts  7.39 us (27%)
  between operations  0.65 us (2%)
    pallas_call x1, Pallas kernels, fused(): pl.pallas_call(functools.partial(kernel, n_grp, n_sub), out_shape=(out, o...  19 us
    unnamed x14, local copies, waits for them, and re-layouts  7.39 us

profile of v1, /device:TPU:0, one launch (start us, length us, event | category | flops | bytes accessed | tf_op | source)
XLA Modules:
  0.0 27.0 jit_solution(13321258418133917925)
XLA Ops:
  0.6 0.0 copy-start
  0.6 1.6 %copy-done = bf16[1,1024,1024]{2,1,0:T(8,128)(2,1)S(1)} copy-done((bf16[1,1024,1024]{2,1,0:T(8,128)(2,1)S(1)}, bf16[1,1024,1024]{2,1,0:T(8,128)(2,1)}, u32[]{:S(2)}) %copy-start) | copy-done | bytes 2097176
  2.2 0.0 copy-start.1
  2.2 1.6 %copy-done.1 = bf16[1,1024,1024]{2,1,0:T(8,128)(2,1)S(1)} copy-done((bf16[1,1024,1024]{2,1,0:T(8,128)(2,1)S(1)}, bf16[1,1024,1024]{2,1,0:T(8,128)(2,1)}, u32[]{:S(2)}) %copy-start.1) | copy-done | bytes 2097176
  3.8 0.0 copy-start.2
  3.8 0.9 %copy-done.2 = f32[1,24,1024]{2,1,0:T(8,128)S(1)} copy-done((f32[1,24,1024]{2,1,0:T(8,128)S(1)}, f32[1,24,1024]{2,1,0:T(8,128)}, u32[]{:S(2)}) %copy-start.2) | copy-done | bytes 98328
  4.7 0.0 copy-start.3
  4.7 0.8 %copy-done.3 = f32[1,8,1024]{2,1,0:T(8,128)S(1)} copy-done((f32[1,8,1024]{2,1,0:T(8,128)S(1)}, f32[1,8,1024]{2,1,0:T(8,128)}, u32[]{:S(2)}) %copy-start.3) | copy-done | bytes 32792
  5.5 0.0 copy-start.4
  5.5 0.7 %copy-done.4 = f32[4,128]{1,0:T(4,128)S(1)} copy-done((f32[4,128]{1,0:T(4,128)S(1)}, f32[4,128]{1,0:T(4,128)}, u32[]{:S(2)}) %copy-start.4) | copy-done | bytes 2072
  6.1 0.0 copy-start.5
  6.2 0.7 %copy-done.5 = s32[1,24]{1,0:T(1,128)S(1)} copy-done((s32[1,24]{1,0:T(1,128)S(1)}, s32[1,24]{1,0:T(1,128)}, u32[]{:S(2)}) %copy-start.5) | copy-done | bytes 120
  6.8 19.0 %shard_map.77 = (f32[1,8,1024]{2,1,0:T(8,128)S(1)}, f32[1,8,1024]{2,1,0:T(8,128)S(1)}) custom-call(f32[1,8,1024]{2,1,0:T(8,128)S(1)} %copy-done.3, bf16[1,1024,1024]{2,1,0:T(8,128)(2,1)S(1)} %copy-done, bf16[1,1024,1024]{2,1,0:T(8,128)(2,1)S(1)} %copy-done.1, f32[1,24,1024]{2,1,0:T(8,128)S(1)} %copy-done.2, s32[1,24]{1,0:T(1,128)S(1)} %copy-done.5, ...), custom_call_target="tpu_custom_call" | custom-call | tf_op jit(solution)/shard_map/pallas_call | solution.py:304
  25.8 0.6 %copy.10 = f32[1,8,1024]{2,1,0:T(8,128)} copy(f32[1,8,1024]{2,1,0:T(8,128)S(1)} %get-tuple-element.4) | data formatting | bytes 65536
  26.4 0.6 %copy.11 = f32[1,8,1024]{2,1,0:T(8,128)} copy(f32[1,8,1024]{2,1,0:T(8,128)S(1)} %get-tuple-element.5) | data formatting | bytes 65536
Async XLA Ops:
  0.6 1.6 %copy-start = (bf16[1,1024,1024]{2,1,0:T(8,128)(2,1)S(1)}, bf16[1,1024,1024]{2,1,0:T(8,128)(2,1)}, u32[]{:S(2)}) copy-start(bf16[1,1024,1024]{2,1,0:T(8,128)(2,1)} %schur_hbm.1) | copy-start | bytes 6291460
  2.2 1.6 %copy-start.1 = (bf16[1,1024,1024]{2,1,0:T(8,128)(2,1)S(1)}, bf16[1,1024,1024]{2,1,0:T(8,128)(2,1)}, u32[]{:S(2)}) copy-start(bf16[1,1024,1024]{2,1,0:T(8,128)(2,1)} %neumann_hbm.1) | copy-start | bytes 6291460
  3.8 0.9 %copy-start.2 = (f32[1,24,1024]{2,1,0:T(8,128)S(1)}, f32[1,24,1024]{2,1,0:T(8,128)}, u32[]{:S(2)}) copy-start(f32[1,24,1024]{2,1,0:T(8,128)} %basis_hbm.1) | copy-start | bytes 294916
  4.7 0.8 %copy-start.3 = (f32[1,8,1024]{2,1,0:T(8,128)S(1)}, f32[1,8,1024]{2,1,0:T(8,128)}, u32[]{:S(2)}) copy-start(f32[1,8,1024]{2,1,0:T(8,128)} %loads_hbm.1) | copy-start | bytes 98308
  5.5 0.7 %copy-start.4 = (f32[4,128]{1,0:T(4,128)S(1)}, f32[4,128]{1,0:T(4,128)}, u32[]{:S(2)}) copy-start(f32[4,128]{1,0:T(4,128)} %inverse_hbm.1) | copy-start | bytes 6148
  6.1 0.7 %copy-start.5 = (s32[1,24]{1,0:T(1,128)S(1)}, s32[1,24]{1,0:T(1,128)}, u32[]{:S(2)}) copy-start(s32[1,24]{1,0:T(1,128)} %index_hbm.1) | copy-start | bytes 292

commit v2 on v1

--- a/solution.py
+++ b/solution.py
@@ -35,13 +35,12 @@
 def kernel(
     n_grp, n_sub,
     loads_hbm, schur_hbm, neumann_hbm, basis_hbm, index_hbm, inverse_hbm,
-    solution_hbm, residual_hbm,
+    solution, residual,
     loads, schur, neumann, basis, index, inverse_parts, inverse,
     loads_in, basis_in, index_in, part_in, result_in,
-    e_high, e_low, h_high, h_low, part, result, solution, residual,
-    terms, terms_grp, group_terms, terms_sub,
-    local_sem, halo_send, halo_recv, grp_send, grp_recv, sub_send, sub_recv,
-    inv_sub_send, inv_sub_recv, inv_grp_send, inv_grp_recv,
+    e_high, e_low, h_high, h_low, part, result,
+    terms, terms_in,
+    local_sem, halo_send, halo_recv, terms_send, terms_recv, inv_send, inv_recv,
 ):
     width = loads.shape[1]
     coarse = inverse.shape[0]
@@ -50,16 +49,15 @@
     b = lax.axis_index("sub")
     grp_peers = [lax.rem(g + k, n_grp) for k in range(1, n_grp)]
     sub_peers = [lax.rem(b + k, n_sub) for k in range(1, n_sub)]
+    peers = [(i, j) for i in [g] + grp_peers for j in [b] + sub_peers][1:]
     has_left = b > 0
     has_right = b < n_sub - 1
     first = pl.ds(0, RIM)
     last = pl.ds(width - RIM, RIM)
 
     barrier = pltpu.get_barrier_semaphore()
-    for peer in sub_peers:
-        pl.semaphore_signal(barrier, inc=1, device_id=(g, peer), device_id_type=MESH)
-    for peer in grp_peers:
-        pl.semaphore_signal(barrier, inc=1, device_id=(peer, b), device_id_type=MESH)
+    for peer in peers:
+        pl.semaphore_signal(barrier, inc=1, device_id=peer, device_id_type=MESH)
 
     def fetch(source, target, at):
         copy = pltpu.make_async_copy(source, target, local_sem.at[at])
@@ -117,18 +115,18 @@
     result_halo = halo(result.at[:, first], result.at[:, last], result_in, 4)
 
     loads_copy.wait()
-    pl.semaphore_wait(barrier, n_grp + n_sub - 2)
+    pl.semaphore_wait(barrier, n_grp * n_sub - 1)
     loads_halo[0]()
     index_copy.wait()
     index_halo[0]()
     basis_copy.wait()
     basis_halo[0]()
     inverse_copy.wait()
-    inv_sub = [
-        remote(inverse_parts.at[g, b], inverse_parts.at[g, b], inv_sub_send.at[k], inv_sub_recv.at[k], (g, peer))
-        for k, peer in enumerate(sub_peers)
+    inv_all = [
+        remote(inverse_parts.at[g, b], inverse_parts.at[g, b], inv_send.at[k], inv_recv.at[k], peer)
+        for k, peer in enumerate(peers)
     ]
-    for copy in inv_sub:
+    for copy in inv_all:
         copy.start()
 
     def expand(index_row, functions):
@@ -156,11 +154,10 @@
     force = assembled(loads[...], loads_in)
     weighted = weights * force
     terms[...] = thin_dot(weighted, e_high[...], e_low[...], NT)
-    to_grp = [
-        remote(terms, terms_grp.at[k], grp_send.at[k], grp_recv.at[k], (peer, b))
-        for k, peer in enumerate(grp_peers)
+    to_all = [
+        remote(terms, terms_in.at[k], terms_send, terms_recv, peer) for k, peer in enumerate(peers)
     ]
-    for copy in to_grp:
+    for copy in to_all:
         copy.start()
 
     neumann_copy.wait()
@@ -174,27 +171,6 @@
     neumann_columns(0, RIM)
     neumann_columns(width - RIM, RIM)
     part_halo[0]()
-
-    total = terms[...]
-    for k, copy in enumerate(to_grp):
-        copy.wait_recv()
-        total = total + terms_grp[k]
-    group_terms[...] = total
-    to_sub = [
-        remote(group_terms, terms_sub.at[k], sub_send.at[k], sub_recv.at[k], (g, peer))
-        for k, peer in enumerate(sub_peers)
-    ]
-    for copy in to_sub:
-        copy.start()
-
-    for copy in inv_sub:
-        copy.wait_recv()
-    inv_grp = [
-        remote(inverse_parts.at[g], inverse_parts.at[g], inv_grp_send.at[k], inv_grp_recv.at[k], (peer, b))
-        for k, peer in enumerate(grp_peers)
-    ]
-    for copy in inv_grp:
-        copy.start()
 
     neumann_columns(RIM, width - 2 * RIM)
 
@@ -204,7 +180,7 @@
     from_left = own[:, :RIM] + 0.5 * expand(index_in[0], basis_in[0])
     from_right = own[:, width - RIM :] + 0.5 * expand(index_in[1], basis_in[1])
     f_high, f_low = split(jnp.concatenate([from_left, own[:, RIM : width - RIM], from_right], axis=1))
-    for copy in inv_grp:
+    for copy in inv_all:
         copy.wait_recv()
     for i in range(n_grp):
         for j in range(n_sub):
@@ -219,14 +195,10 @@
     part_halo[1]()
     base = assembled(part[...], part_in)
 
-    total = group_terms[...]
-    for k, copy in enumerate(to_sub):
-        copy.wait_recv()
-        total = total + terms_sub[k]
+    pltpu.make_async_copy(terms_in, terms_in, terms_recv).wait()
+    total = terms[...] + jnp.sum(terms_in[...], axis=0)
     found = base + thin_dot(total, h_high[...], h_low[...])
-    solution[...] = found
-    solution_copy = pltpu.make_async_copy(solution, solution_hbm.at[0], local_sem.at[6])
-    solution_copy.start()
+    solution[0] = found
 
     schur_copy.wait()
     rounded_solution = found.astype(BF16)
@@ -240,19 +212,26 @@
     result[:, :RIM] = low_rim
     result[:, width - RIM :] = high_rim
     result_halo[0]()
-    residual[:, RIM : width - RIM] = force[:, RIM : width - RIM] - schur_columns(RIM, width - 2 * RIM)
-    for copy in inv_sub + inv_grp + to_grp + to_sub:
+    residual[0, :, RIM : width - RIM] = force[:, RIM : width - RIM] - schur_columns(RIM, width - 2 * RIM)
+    for copy in inv_all + to_all:
         copy.wait_send()
     for each in (loads_halo, basis_halo, index_halo, part_halo):
         each[2]()
     result_halo[1]()
-    residual[:, :RIM] = force[:, :RIM] - (low_rim + result_in[0])
-    residual[:, width - RIM :] = force[:, width - RIM :] - (high_rim + result_in[1])
-    residual_copy = pltpu.make_async_copy(residual, residual_hbm.at[0], local_sem.at[7])
-    residual_copy.start()
+    residual[0, :, :RIM] = force[:, :RIM] - (low_rim + result_in[0])
+    residual[0, :, width - RIM :] = force[:, width - RIM :] - (high_rim + result_in[1])
     result_halo[2]()
-    solution_copy.wait()
-    residual_copy.wait()
+
+
+def store(solution, residual, solution_hbm, residual_hbm, sems):
+    copies = [
+        pltpu.make_async_copy(solution, solution_hbm, sems.at[0]),
+        pltpu.make_async_copy(residual, residual_hbm, sems.at[1]),
+    ]
+    for copy in copies:
+        copy.start()
+    for copy in copies:
+        copy.wait()
 
 
 def fused(loads, schur, neumann, basis, coarse_index, coarse_inverse):
@@ -282,35 +261,37 @@
         pltpu.VMEM((coarse, width), BF16),
         field,
         field,
-        field,
-        field,
         pltpu.VMEM((cases, coarse), F32),
-        pltpu.VMEM((n_grp - 1, cases, coarse), F32),
-        pltpu.VMEM((cases, coarse), F32),
-        pltpu.VMEM((n_sub - 1, cases, coarse), F32),
-        dma((8,)),
+        pltpu.VMEM((n_grp * n_sub - 1, cases, coarse), F32),
+        dma((6,)),
         dma((5, 2)),
         dma((5, 2)),
-        dma((n_grp - 1,)),
-        dma((n_grp - 1,)),
-        dma((n_sub - 1,)),
-        dma((n_sub - 1,)),
-        dma((n_sub - 1,)),
-        dma((n_sub - 1,)),
-        dma((n_grp - 1,)),
-        dma((n_grp - 1,)),
+        dma,
+        dma,
+        dma((n_grp * n_sub - 1,)),
+        dma((n_grp * n_sub - 1,)),
     ]
     out = jax.ShapeDtypeStruct(loads.shape, F32)
-    return pl.pallas_call(
+    in_hbm = pl.BlockSpec(memory_space=pltpu.HBM)
+    in_vmem = pl.BlockSpec(memory_space=pltpu.VMEM)
+    found = pl.pallas_call(
         functools.partial(kernel, n_grp, n_sub),
-        out_shape=(out, out),
-        in_specs=[pl.BlockSpec(memory_space=pl.ANY)] * 6,
-        out_specs=(pl.BlockSpec(memory_space=pl.ANY),) * 2,
+        out_shape=(pltpu.VMEM(loads.shape, F32),) * 2,
+        in_specs=[in_hbm] * 6,
+        out_specs=(in_vmem, in_vmem),
         scratch_shapes=scratch,
         compiler_params=pltpu.CompilerParams(
-            collective_id=0, has_side_effects=True, vmem_limit_bytes=48 << 20
+            collective_id=0, has_side_effects=True
         ),
     )(loads, schur, neumann, basis, coarse_index, coarse_inverse)
+    return pl.pallas_call(
+        store,
+        out_shape=(out, out),
+        in_specs=[in_vmem] * 2,
+        out_specs=(in_hbm, in_hbm),
+        scratch_shapes=[dma((2,))],
+        compiler_params=pltpu.CompilerParams(vmem_limit_bytes=1 << 20),
+    )(*found)
 
 
 def with_halo(x, sides, width):

time: 27.3 us -> 19.9 us (0.73)
  local copies, waits for them, and re-layouts: 7.39 us -> 0 us
    unnamed x14 -> x0, local copies, waits for them, and re-layouts: 7.39 us -> none
    pallas_call x1 -> x2, Pallas kernels: 19 us -> 19.1 us  [the longest x1 18.4 us: fused(): pl.pallas_call(functools.partial(kernel, n_grp, n_sub), out_shape=(pltpu....]
where the time goes in v2:
time: 19.9 us; the launch traced here: 19.7 us
  Pallas kernels  19.1 us (96%)
  between operations  0.64 us (3%)
    pallas_call x1, Pallas kernels, fused(): pl.pallas_call(functools.partial(kernel, n_grp, n_sub), out_shape=(pltpu....  18.4 us
    pallas_call x1, Pallas kernels, fused(): pl.pallas_call(store, out_shape=(out, out), in_specs=[in_vmem] * 2, out_s...  0.65 us

profile of v2, /device:TPU:0, one launch (start us, length us, event | category | flops | bytes accessed | tf_op | source)
XLA Modules:
  0.0 19.7 jit_solution(11759449012255599506)
XLA Ops:
  0.6 18.4 %shard_map.77 = (f32[1,8,1024]{2,1,0:T(8,128)S(1)}, f32[1,8,1024]{2,1,0:T(8,128)S(1)}) custom-call(f32[1,8,1024]{2,1,0:T(8,128)} %loads_hbm.1, bf16[1,1024,1024]{2,1,0:T(8,128)(2,1)} %schur_hbm.1, bf16[1,1024,1024]{2,1,0:T(8,128)(2,1)} %neumann_hbm.1, f32[1,24,1024]{2,1,0:T(8,128)} %basis_hbm.1, s32[1,24]{1,0:T(1,128)} %index_hbm.1, f32[4,128]{1,0:T(4,128)} %inverse_hbm.1), custom_call_target="tpu_custom_call" | custom-call | tf_op jit(solution)/shard_map/pallas_call | solution.py:277
  19.1 0.6 %shard_map.78 = (f32[1,8,1024]{2,1,0:T(8,128)}, f32[1,8,1024]{2,1,0:T(8,128)}) custom-call(f32[1,8,1024]{2,1,0:T(8,128)S(1)} %get-tuple-element.4.solution, f32[1,8,1024]{2,1,0:T(8,128)S(1)} %get-tuple-element.5.residual), custom_call_target="tpu_custom_call" | custom-call | tf_op jit(solution)/shard_map/pallas_call | solution.py:287

commit v3 on v2

--- a/solution.py
+++ b/solution.py
@@ -122,11 +122,11 @@
     basis_copy.wait()
     basis_halo[0]()
     inverse_copy.wait()
-    inv_all = [
-        remote(inverse_parts.at[g, b], inverse_parts.at[g, b], inv_send.at[k], inv_recv.at[k], peer)
-        for k, peer in enumerate(peers)
-    ]
-    for copy in inv_all:
+    inv_sub = [
+        remote(inverse_parts.at[g, b], inverse_parts.at[g, b], inv_send.at[k], inv_recv.at[k], (g, peer))
+        for k, peer in enumerate(sub_peers)
+    ]
+    for copy in inv_sub:
         copy.start()
 
     def expand(index_row, functions):
@@ -158,6 +158,18 @@
         remote(terms, terms_in.at[k], terms_send, terms_recv, peer) for k, peer in enumerate(peers)
     ]
     for copy in to_all:
+        copy.start()
+
+    for copy in inv_sub:
+        copy.wait_recv()
+    inv_grp = [
+        remote(
+            inverse_parts.at[g], inverse_parts.at[g],
+            inv_send.at[n_sub - 1 + k], inv_recv.at[n_sub - 1 + k], (peer, b),
+        )
+        for k, peer in enumerate(grp_peers)
+    ]
+    for copy in inv_grp:
         copy.start()
 
     neumann_copy.wait()
@@ -180,7 +192,7 @@
     from_left = own[:, :RIM] + 0.5 * expand(index_in[0], basis_in[0])
     from_right = own[:, width - RIM :] + 0.5 * expand(index_in[1], basis_in[1])
     f_high, f_low = split(jnp.concatenate([from_left, own[:, RIM : width - RIM], from_right], axis=1))
-    for copy in inv_all:
+    for copy in inv_grp:
         copy.wait_recv()
     for i in range(n_grp):
         for j in range(n_sub):
@@ -213,7 +225,7 @@
     result[:, width - RIM :] = high_rim
     result_halo[0]()
     residual[0, :, RIM : width - RIM] = force[:, RIM : width - RIM] - schur_columns(RIM, width - 2 * RIM)
-    for copy in inv_all + to_all:
+    for copy in inv_sub + inv_grp + to_all:
         copy.wait_send()
     for each in (loads_halo, basis_halo, index_halo, part_halo):
         each[2]()
@@ -268,8 +280,8 @@
         dma((5, 2)),
         dma,
         dma,
-        dma((n_grp * n_sub - 1,)),
-        dma((n_grp * n_sub - 1,)),
+        dma((n_grp + n_sub - 2,)),
+        dma((n_grp + n_sub - 2,)),
     ]
     out = jax.ShapeDtypeStruct(loads.shape, F32)
     in_hbm = pl.BlockSpec(memory_space=pltpu.HBM)

time: 19.9 us -> 19.2 us (0.965)
  Pallas kernels: 19.1 us -> 18.4 us
    pallas_call x1, Pallas kernels: 18.4 us -> 17.8 us  [fused(): pl.pallas_call(functools.partial(kernel, n_grp, n_sub), out_shape=(pltpu....]
where the time goes in v3:
time: 19.2 us; the launch traced here: 19.1 us
  Pallas kernels  18.4 us (96%)
  between operations  0.64 us (3%)
    pallas_call x1, Pallas kernels, fused(): pl.pallas_call(functools.partial(kernel, n_grp, n_sub), out_shape=(pltpu....  17.8 us
    pallas_call x1, Pallas kernels, fused(): pl.pallas_call(store, out_shape=(out, out), in_specs=[in_vmem] * 2, out_s...  0.65 us

profile of v3, /device:TPU:0, one launch (start us, length us, event | category | flops | bytes accessed | tf_op | source)
XLA Modules:
  0.0 19.1 jit_solution(16800593012559889315)
XLA Ops:
  0.6 17.8 %shard_map.77 = (f32[1,8,1024]{2,1,0:T(8,128)S(1)}, f32[1,8,1024]{2,1,0:T(8,128)S(1)}) custom-call(f32[1,8,1024]{2,1,0:T(8,128)} %loads_hbm.1, bf16[1,1024,1024]{2,1,0:T(8,128)(2,1)} %schur_hbm.1, bf16[1,1024,1024]{2,1,0:T(8,128)(2,1)} %neumann_hbm.1, f32[1,24,1024]{2,1,0:T(8,128)} %basis_hbm.1, s32[1,24]{1,0:T(1,128)} %index_hbm.1, f32[4,128]{1,0:T(4,128)} %inverse_hbm.1), custom_call_target="tpu_custom_call" | custom-call | tf_op jit(solution)/shard_map/pallas_call | solution.py:289
  18.4 0.6 %shard_map.78 = (f32[1,8,1024]{2,1,0:T(8,128)}, f32[1,8,1024]{2,1,0:T(8,128)}) custom-call(f32[1,8,1024]{2,1,0:T(8,128)S(1)} %get-tuple-element.4.solution, f32[1,8,1024]{2,1,0:T(8,128)S(1)} %get-tuple-element.5.residual), custom_call_target="tpu_custom_call" | custom-call | tf_op jit(solution)/shard_map/pallas_call | solution.py:299
